TPU v7x, 32 devices: a whole 2x2x4 slice. The times are simulated.
32 devices in a mesh: groups: 2 (over y), blk: 4 (over z), col: 2 (over x), rep: 2 (over core).
Axes of the slice: x: 2, y: 2, z: 4, core: 2. Of those that a mesh axis runs over, the one named last changes fastest.
Arguments:
- row_factors: bfloat16 [16384, 256], P(('groups', 'blk', 'rep')), parts along dimension 0, may hold values from -1.5 to 1.5
- col_factors: bfloat16 [4096, 256], P(('groups', 'blk', 'col')), parts along dimension 0, may hold values from -1.5 to 1.5
- counts: int32 [16384, 4, 512], P(('groups', 'blk', 'rep'), None, 'col'), parts along dimension 0, may hold values from 0 to 1024, as said below
- row_margin: int32 [16384], P(('groups', 'blk', 'rep')), parts along dimension 0, may hold values from 100 to 7996
- col_margin: int32 [4096], P('groups'), parts along dimension 0, may hold values from 10000 to 99999
Outputs:
- row_grad: float32 [16384, 256], P(('groups', 'blk', 'rep')), parts along dimension 0
- col_grad: float32 [4096, 256], P(('groups', 'blk', 'col')), parts along dimension 0
There are 2 independent parts, one for each index of `groups`. A program takes and returns all parts, laid end to end along the dimension named above; each array names one. Nothing has to cross between parts.
Inputs may be any that keep to these rules, and one draw needn't show every extreme that they name: `counts`: zero marks pairs never seen together.
All inputs are finite; a program needn't handle non-finite values.
Results may differ from a plain program's by a relative error of at most 0.0027.
Values may be sent and summed in bfloat16 or wider, within the bound.
A program may use at most 64 MiB of HBM per device.

v0:
```python
import jax
import jax.numpy as jnp
from jax import lax
from jax.sharding import PartitionSpec as P


def passed_along(value, axis, by):
    devices = lax.axis_size(axis)
    return lax.ppermute(value, axis, [(i, (i + by) % devices) for i in range(devices)])


def per_device(row_factors, col_factors, counts, row_margin, col_margin):
    col_piece = col_factors.shape[0]
    step_count = counts.shape[1]
    half_steps = step_count // 2
    cycle_size = lax.axis_size("blk")
    block_cols = col_piece * lax.axis_size("col")
    cycle_index = lax.axis_index("blk")
    col_index = lax.axis_index("col")
    grand_sum = lax.psum(jnp.sum(row_margin.astype(jnp.float32)), ("blk", "rep"))
    row_base = jnp.log(grand_sum) - jnp.log(row_margin.astype(jnp.float32))
    col_logs = jnp.log(col_margin.astype(jnp.float32))
    loss_scale = float(step_count * block_cols) ** (-0.5)
    factors = passed_along(col_factors, "blk", 1 - half_steps)
    row_total = None
    carried = None
    for position in range(step_count):
        offset = half_steps - 1 - position
        carried_factors = factors
        col_block = (cycle_index + offset) % cycle_size
        first_col = col_block * block_cols + col_index * col_piece
        col_log_part = lax.dynamic_slice_in_dim(col_logs, first_col, col_piece)
        tile_counts = counts[:, offset + half_steps, :]
        tile_score = lax.dot_general(
            row_factors,
            carried_factors,
            (((1,), (1,)), ((), ())),
            preferred_element_type=jnp.float32,
        )
        tile_base = row_base[:, None] - col_log_part[None, :]
        counted = tile_counts.astype(jnp.float32)
        target = jnp.log(jnp.maximum(counted, 1.0)) + tile_base
        confidence = 0.1 + 0.25 * jnp.sqrt(counted)
        tile_slope = jnp.where(
            tile_counts > 0,
            confidence * (tile_score - target),
            jax.nn.sigmoid(tile_score - tile_base),
        )
        tile_slope = (tile_slope * loss_scale).astype(jnp.bfloat16)
        row_part = jnp.dot(tile_slope, carried_factors, preferred_element_type=jnp.float32)
        col_part = lax.dot_general(
            tile_slope, row_factors, (((0,), (0,)), ((), ())), preferred_element_type=jnp.float32
        )
        row_part, col_part = (row_part, col_part)
        row_total = row_part if row_total is None else row_total + row_part
        carried = col_part if carried is None else carried + col_part
        if position + 1 < step_count:
            factors = passed_along(factors, "blk", 1)
            carried = passed_along(carried, "blk", 1)
    col_total = passed_along(carried, "blk", -half_steps)
    row_grad = lax.psum(row_total, "col")
    col_grad = lax.psum(col_total, "rep")
    return (row_grad, col_grad)


def solution(mesh):
    in_specs = (
        P(("groups", "blk", "rep"), None),
        P(("groups", "blk", "col"), None),
        P(("groups", "blk", "rep"), None, "col"),
        P(("groups", "blk", "rep")),
        P("groups"),
    )
    out_specs = (P(("groups", "blk", "rep"), None), P(("groups", "blk", "col"), None))
    return jax.shard_map(
        per_device, mesh=mesh, in_specs=in_specs, out_specs=out_specs, check_vma=False
    )
```

profile of v0, /device:TPU:0, one launch (start us, length us, event | category | flops | bytes accessed | tf_op | source)
XLA Modules:
  0.0 177.1 jit_solution(651517708919845168)
XLA Ops:
  7.2 0.0 copy-start
  7.2 0.0 all-reduce.5.cloned.1.call-start
  7.2 1.3 convert_reduce_fusion
  8.6 5.0 %collective-permute-start = (bf16[256,256]{1,0:T(8,128)(2,1)}, bf16[256,256]{1,0:T(8,128)(2,1)S(1)}, u32[]{:S(2)}, u32[]{:S(2)}) collective-permute-start(bf16[256,256]{1,0:T(8,128)(2,1)} %param.6), channel_id=1, source_target_pairs={{0,12},{4,0},{8,4},{12,8},{1,13},{5,1},{9,5},{13,9},{2,14},{6,2},{... | collective-permute-start | bytes 393224 | tf_op jit(solution)/shard_map/ppermute | solution.py:9
  13.6 15.0 %psum.21 = f32[]{:T(128)} all-reduce(f32[]{:T(128)} %convert_reduce_fusion), channel_id=1, replica_groups=mesh['groups'=2,'blk'=4,'col'=2,'rep'=2] {'blk','rep'}, use_global_device_ids=true, to_apply=%region_1.0 | all-reduce | flops 1 | bytes 8 | tf_op jit(solution)/shard_map/psum | solution.py:20
  29.3 0.7 convert_log_fusion
  30.0 11.5 %fusion.36 = (s32[1024,1,256]{2,1,0:T(1,128)S(1)}, s32[1024,1,256]{2,1,0:T(1,128)S(1)}, s32[1024,1,256]{2,1,0:T(1,128)}, s32[1024,1,256]{2,1,0:T(1,128)}) fusion(s32[1024,4,256]{2,1,0:T(4,128)} %param.7), kind=kLoop, calls=%fused_computation.51 | loop fusion | bytes 8388608 | tf_op jit(solution)/shard_map/slice | solution.py:33
  41.5 0.0 copy-done.4
  41.5 0.0 copy-start.1
  41.5 0.0 copy-start.2
  41.6 0.1 fusion.37
  41.6 0.0 collective-permute-done
  41.7 0.0 collective-permute-start.1
  41.7 0.0 copy-done
  41.7 0.3 fusion.38
  42.0 6.4 %collective-permute-done.1 = bf16[256,256]{1,0:T(8,128)(2,1)S(1)} collective-permute-done((bf16[256,256]{1,0:T(8,128)(2,1)S(1)}, bf16[256,256]{1,0:T(8,128)(2,1)S(1)}, u32[]{:S(2)}, u32[]{:S(2)}) %collective-permute-start.1) | collective-permute-done | bytes 131104 | tf_op jit(solution)/shard_map/ppermute | solution.py:9
  48.4 0.0 collective-permute-start.2
  48.4 0.3 fusion.40
  48.8 6.4 %collective-permute-done.2 = bf16[256,256]{1,0:T(8,128)(2,1)S(1)} collective-permute-done((bf16[256,256]{1,0:T(8,128)(2,1)S(1)}, bf16[256,256]{1,0:T(8,128)(2,1)S(1)}, u32[]{:S(2)}, u32[]{:S(2)}) %collective-permute-start.2) | collective-permute-done | bytes 131104 | tf_op jit(solution)/shard_map/ppermute | solution.py:9
  55.2 0.0 collective-permute-start.3
  55.2 0.3 fusion.41
  55.5 6.4 %collective-permute-done.3 = bf16[256,256]{1,0:T(8,128)(2,1)S(1)} collective-permute-done((bf16[256,256]{1,0:T(8,128)(2,1)S(1)}, bf16[256,256]{1,0:T(8,128)(2,1)S(1)}, u32[]{:S(2)}, u32[]{:S(2)}) %collective-permute-start.3) | collective-permute-done | bytes 131104 | tf_op jit(solution)/shard_map/ppermute | solution.py:9
  62.0 0.0 copy-done.1
  62.0 4.3 %fusion.31 = (bf16[1024,256]{1,0:T(8,128)(2,1)S(1)}, bf16[1024,256]{1,0:T(8,128)(2,1)S(1)}, bf16[1024,256]{1,0:T(8,128)(2,1)S(1)}, bf16[1024,256]{1,0:T(8,128)(2,1)S(1)}) fusion(s32[1024,1,256]{2,1,0:T(1,128)S(1)} %get-tuple-element.2, f32[256]{0:T(256)S(1)} %get-tuple-element.6, f32[1024]{0:T(1024)S(1)} %log_subtract_fusion, f32[1024,256]{1,0:T(8,128)S(1)} %fusion.40, ...), kind=kOutput, calls=%fused_computation.43 | convolution fusion | flops 150994944 | bytes 10100736 | tf_op jit(solution)/shard_map/dot_general | solution.py:34
  66.3 0.3 fusion.42
  66.6 0.1 collective-permute-start.4
  66.7 8.8 %collective-permute-done.4 = f32[256,256]{1,0:T(8,128)S(1)} collective-permute-done((f32[256,256]{1,0:T(8,128)S(1)}, f32[256,256]{1,0:T(8,128)S(1)}, u32[]{:S(2)}, u32[]{:S(2)}) %collective-permute-start.4) | collective-permute-done | bytes 262176 | tf_op jit(solution)/shard_map/ppermute | solution.py:9
  75.5 0.3 convolution_add_fusion.3
  75.8 0.1 collective-permute-start.5
  75.9 0.3 fusion.39
  76.2 0.3 fusion.43
  76.5 9.7 %collective-permute-done.5 = f32[256,256]{1,0:T(8,128)S(1)} collective-permute-done((f32[256,256]{1,0:T(8,128)S(1)}, f32[256,256]{1,0:T(8,128)S(1)}, u32[]{:S(2)}, u32[]{:S(2)}) %collective-permute-start.5) | collective-permute-done | bytes 262176 | tf_op jit(solution)/shard_map/ppermute | solution.py:9
  86.2 0.1 collective-permute-start.6
  86.3 0.3 convolution_add_fusion.2
  86.6 0.3 fusion.44
  86.9 7.6 %collective-permute-done.6 = f32[256,256]{1,0:T(8,128)S(1)} collective-permute-done((f32[256,256]{1,0:T(8,128)S(1)}, f32[256,256]{1,0:T(8,128)S(1)}, u32[]{:S(2)}, u32[]{:S(2)}) %collective-permute-start.6) | collective-permute-done | bytes 262176 | tf_op jit(solution)/shard_map/ppermute | solution.py:9
  94.6 0.1 collective-permute-start.7
  94.7 0.3 convolution_add_fusion.1
  95.0 9.8 %collective-permute-done.7 = f32[256,256]{1,0:T(8,128)S(1)} collective-permute-done((f32[256,256]{1,0:T(8,128)S(1)}, f32[256,256]{1,0:T(8,128)S(1)}, u32[]{:S(2)}, u32[]{:S(2)}) %collective-permute-start.7) | collective-permute-done | bytes 262176 | tf_op jit(solution)/shard_map/ppermute | solution.py:9
  104.7 0.7 copy-done.3
  105.4 0.0 all-reduce.5.cloned.1.call-update
  105.5 0.0 all-reduce.3.cloned.1.call-start
  105.5 1.3 convolution_add_fusion
  106.8 0.0 all-reduce.3.cloned.1.call-update
  106.8 15.3 %all-reduce.5.cloned.1.call-done = f32[256,256]{1,0:T(8,128)} async-done(((f32[256,256]{1,0:T(8,128)}), f32[256,256]{1,0:T(8,128)}) %all-reduce.5.cloned.1.call-update) | async-done | bytes 262160 | tf_op jit(solution)/shard_map/psum | solution.py:62
  122.1 44.2 %all-reduce.3.cloned.1.call-done = f32[1024,256]{1,0:T(8,128)} async-done(((f32[1024,256]{1,0:T(8,128)}), f32[1024,256]{1,0:T(8,128)}) %all-reduce.3.cloned.1.call-update) | async-done | bytes 1048592 | tf_op jit(solution)/shard_map/psum | solution.py:61
  166.3 2.3 %copy.22 = f32[1024,256]{1,0:T(8,128)} copy(f32[1024,256]{1,0:T(8,128)} %all-reduce.3.cloned.1.call-done) | data formatting | bytes 2097152
  168.5 1.7 copy.23
  (6 shorter events, 0.1 us)
Async XLA Ops:
  7.2 34.5 %copy-start = (bf16[1024,256]{1,0:T(8,128)(2,1)S(1)}, bf16[1024,256]{1,0:T(8,128)(2,1)}, u32[]{:S(2)}) copy-start(bf16[1024,256]{1,0:T(8,128)(2,1)} %param.5) | copy-start | bytes 1572868
  7.2 114.9 %all-reduce.5.cloned.1.call-start = ((), (), s32[]{:S(2)}) async-start(), calls=%async_computation.1 | async-start | bytes 524288 | tf_op jit(solution)/shard_map/psum | solution.py:62
  8.6 33.1 %collective-permute-start = (bf16[256,256]{1,0:T(8,128)(2,1)}, bf16[256,256]{1,0:T(8,128)(2,1)S(1)}, u32[]{:S(2)}, u32[]{:S(2)}) collective-permute-start(bf16[256,256]{1,0:T(8,128)(2,1)} %param.6), channel_id=1, source_target_pairs={{0,12},{4,0},{8,4},{12,8},{1,13},{5,1},{9,5},{13,9},{2,14},{6,2},{... | collective-permute-start | bytes 393224 | tf_op jit(solution)/shard_map/ppermute | solution.py:9
  30.0 11.5 %copy-start.4 = (s32[1024]{0:T(1024)S(1)}, s32[1024]{0:T(1024)}, u32[]{:S(2)}) copy-start(s32[1024]{0:T(1024)} %param.8) | copy-start | bytes 12292
  41.5 20.4 %copy-start.1 = (s32[1024,1,256]{2,1,0:T(1,128)S(1)}, s32[1024,1,256]{2,1,0:T(1,128)}, u32[]{:S(2)}) copy-start(s32[1024,1,256]{2,1,0:T(1,128)} %get-tuple-element.4) | copy-start | bytes 3145732
  41.5 20.4 %copy-start.2 = (s32[1024,1,256]{2,1,0:T(1,128)S(1)}, s32[1024,1,256]{2,1,0:T(1,128)}, u32[]{:S(2)}) copy-start(s32[1024,1,256]{2,1,0:T(1,128)} %get-tuple-element.5) | copy-start | bytes 3145732
  41.7 6.8 %collective-permute-start.1 = (bf16[256,256]{1,0:T(8,128)(2,1)S(1)}, bf16[256,256]{1,0:T(8,128)(2,1)S(1)}, u32[]{:S(2)}, u32[]{:S(2)}) collective-permute-start(bf16[256,256]{1,0:T(8,128)(2,1)S(1)} %collective-permute-done), channel_id=1, source_target_pairs={{0,4},{4,8},{8,12},{12,0},{1,5},{5,9},{9,13},{13,1},{2,6},{6,10},{... | collective-permute-start | bytes 393224 | tf_op jit(solution)/shard_map/ppermute | solution.py:9
  48.4 6.8 %collective-permute-start.2 = (bf16[256,256]{1,0:T(8,128)(2,1)S(1)}, bf16[256,256]{1,0:T(8,128)(2,1)S(1)}, u32[]{:S(2)}, u32[]{:S(2)}) collective-permute-start(bf16[256,256]{1,0:T(8,128)(2,1)S(1)} %collective-permute-done.1), channel_id=1, source_target_pairs={{0,4},{4,8},{8,12},{12,0},{1,5},{5,9},{9,13},{13,1},{2,6},{6,10},{... | collective-permute-start | bytes 393224 | tf_op jit(solution)/shard_map/ppermute | solution.py:9
  55.2 6.8 %collective-permute-start.3 = (bf16[256,256]{1,0:T(8,128)(2,1)S(1)}, bf16[256,256]{1,0:T(8,128)(2,1)S(1)}, u32[]{:S(2)}, u32[]{:S(2)}) collective-permute-start(bf16[256,256]{1,0:T(8,128)(2,1)S(1)} %collective-permute-done.2), channel_id=1, source_target_pairs={{0,4},{4,8},{8,12},{12,0},{1,5},{5,9},{9,13},{13,1},{2,6},{6,10},{... | collective-permute-start | bytes 393224 | tf_op jit(solution)/shard_map/ppermute | solution.py:9
  66.6 8.9 %collective-permute-start.4 = (f32[256,256]{1,0:T(8,128)S(1)}, f32[256,256]{1,0:T(8,128)S(1)}, u32[]{:S(2)}, u32[]{:S(2)}) collective-permute-start(f32[256,256]{1,0:T(8,128)S(1)} %fusion.42), channel_id=1, source_target_pairs={{0,4},{4,8},{8,12},{12,0},{1,5},{5,9},{9,13},{13,1},{2,6},{6,10},{... | collective-permute-start | bytes 786440 | tf_op jit(solution)/shard_map/ppermute | solution.py:9
  75.8 10.4 %collective-permute-start.5 = (f32[256,256]{1,0:T(8,128)S(1)}, f32[256,256]{1,0:T(8,128)S(1)}, u32[]{:S(2)}, u32[]{:S(2)}) collective-permute-start(f32[256,256]{1,0:T(8,128)S(1)} %convolution_add_fusion.3), channel_id=1, source_target_pairs={{0,4},{4,8},{8,12},{12,0},{1,5},{5,9},{9,13},{13,1},{2,6},{6,10},{... | collective-permute-start | bytes 786440 | tf_op jit(solution)/shard_map/ppermute | solution.py:9
  86.2 8.3 %collective-permute-start.6 = (f32[256,256]{1,0:T(8,128)S(1)}, f32[256,256]{1,0:T(8,128)S(1)}, u32[]{:S(2)}, u32[]{:S(2)}) collective-permute-start(f32[256,256]{1,0:T(8,128)S(1)} %add.153), channel_id=1, source_target_pairs={{0,4},{4,8},{8,12},{12,0},{1,5},{5,9},{9,13},{13,1},{2,6},{6,10},{... | collective-permute-start | bytes 786440 | tf_op jit(solution)/shard_map/ppermute | solution.py:9
  94.6 10.1 %collective-permute-start.7 = (f32[256,256]{1,0:T(8,128)S(1)}, f32[256,256]{1,0:T(8,128)S(1)}, u32[]{:S(2)}, u32[]{:S(2)}) collective-permute-start(f32[256,256]{1,0:T(8,128)S(1)} %add.154), channel_id=1, source_target_pairs={{0,8},{4,12},{8,0},{12,4},{1,9},{5,13},{9,1},{13,5},{2,10},{6,14},... | collective-permute-start | bytes 786440 | tf_op jit(solution)/shard_map/ppermute | solution.py:9
  104.7 0.7 copy-start.3
  105.5 60.8 %all-reduce.3.cloned.1.call-start = ((), (), s32[]{:S(2)}) async-start(), calls=%async_computation | async-start | bytes 2097152 | tf_op jit(solution)/shard_map/psum | solution.py:61
Sparse Core Ops, SparseCore 0:
  105.6 16.4 all-reduce.4
  125.0 41.2 all-reduce.2
where the time goes:
time: 177 us
  waiting for transfers between devices  115 us (65%)
  local copies, waits for them, and re-layouts  16.2 us (9%)
  blocking collectives  15 us (8%)
  between operations  15 us (8%)
  matrix products  8.77 us (5%)
  starting transfers between devices  5.39 us (3%)
  other arithmetic  2.12 us (1%)
    ppermute x8, waiting for transfers between devices, passed_along(): lax.ppermute(value, axis, [(i, (i + by) % devices) for i in range(devices)])  55.1 us
    psum x1, waiting for transfers between devices, per_device(): row_grad = lax.psum(row_total, 'col')  44.2 us
    psum x1, waiting for transfers between devices, per_device(): col_grad = lax.psum(col_total, 'rep')  15.3 us
    psum x1, blocking collectives, per_device(): lax.psum(jnp.sum(row_margin.astype(jnp.float32)), ('blk', 'rep'))  15 us
    slice x1, local copies, waits for them, and re-layouts, per_device(): tile_counts = counts[:, offset + half_steps, :]  11.5 us
    ppermute x8, starting transfers between devices, passed_along(): lax.ppermute(value, axis, [(i, (i + by) % devices) for i in range(devices)])  5.31 us
    dot_general x4, matrix products, per_device(): lax.dot_general(row_factors, carried_factors, (((1,), (1,)), ((), ())), p...  5.27 us
    unnamed x12, local copies, waits for them, and re-layouts  4.66 us
  transfers between devices with their start and end apart: 10, of which 9 were waited for; matrix products, arithmetic and copies ran while one was open for 9% of the time, Pallas kernels for 0%

commit v1 on v0

v1 whole, which is shorter than its diff:
```python
import functools

import jax
import jax.numpy as jnp
from jax import lax
from jax.experimental import pallas as pl
from jax.experimental.pallas import tpu as pltpu
from jax.sharding import PartitionSpec as P

MESH = pl.DeviceIdType.MESH
F32 = jnp.float32
BF16 = jnp.bfloat16
NT = (((1,), (1,)), ((), ()))
LANES = 128


def kernel(dims, rf_hbm, cf_hbm, cnt_hbm, rm_ref, cm_ref,
           parts, colout,
           rf, cfb, cnt, mar, rft, rb, ncl, racc, rbf, cacc, cin, csum, zout, zin, outv,
           cnt_sem, loc_sem, mar_s, mar_r, cf_s, cf_r, fw_s, fw_r,
           rep_s, rep_r, z_s, z_r, x_s, x_r, own_sem, fin_s, fin_r):
    blks, cols, slots, rchunk = dims
    rows, rank = rf.shape
    piece = cfb.shape[1]
    tiles = piece // LANES
    chunks = rows // rchunk
    half = slots // 2
    hp = piece // 2
    hk = rank // 2
    b = lax.axis_index("blk")
    c = lax.axis_index("col")
    r = lax.axis_index("rep")
    other = 1 - r
    loss_scale = float(slots * piece * cols) ** (-0.5)
    others = sorted([s for s in range(slots) if s != half], key=lambda s: abs(s - half))
    per_chunk = rchunk * tiles * slots

    bar = pltpu.get_barrier_semaphore()
    for d in range(blks):
        for e in range(2):
            if d or e:
                pl.semaphore_signal(bar, inc=1, device_id={"blk": lax.rem(b + d, blks), "rep": lax.rem(r + e, 2)},
                                    device_id_type=MESH)
    for k in range(1, cols):
        pl.semaphore_signal(bar, inc=1, device_id={"col": lax.rem(c + k, cols)}, device_id_type=MESH)

    rf_cp = pltpu.make_async_copy(rf_hbm, rf, loc_sem.at[0])
    rf_cp.start()
    cf_cp = pltpu.make_async_copy(cf_hbm, cfb.at[half], loc_sem.at[1])
    cf_cp.start()
    cnt_cp = []
    for i in range(chunks):
        at = pl.ds(i * per_chunk, per_chunk)
        cp = pltpu.make_async_copy(cnt_hbm.at[at], cnt.at[at], cnt_sem.at[i])
        cp.start()
        cnt_cp.append(cp)
    pl.semaphore_wait(bar, 2 * blks - 1 + cols - 1)

    sends = []
    mar_cp = []
    for d in range(blks):
        for e in range(2):
            if d or e:
                k = d * 2 + e
                cp = pltpu.make_async_remote_copy(
                    src_ref=rm_ref, dst_ref=mar.at[k], send_sem=mar_s.at[k], recv_sem=mar_r.at[k],
                    device_id={"blk": lax.rem(b + d, blks), "rep": lax.rem(r + e, 2)}, device_id_type=MESH)
                cp.start()
                mar_cp.append(cp)
    sends += mar_cp
    my_half = pl.ds(pl.multiple_of(r * hp, hp), hp)
    cf_in = {}
    for s in others:
        cp = pltpu.make_async_remote_copy(
            src_ref=cf_hbm.at[my_half], dst_ref=cfb.at[s, my_half], send_sem=cf_s.at[s], recv_sem=cf_r.at[s],
            device_id={"blk": lax.rem(b - s + half + blks, blks)}, device_id_type=MESH)
        cp.start()
        cf_in[s] = cp
    sends += list(cf_in.values())

    lrm = jnp.log(rm_ref[...].astype(F32))
    for g in range(rows // LANES):
        rb[pl.ds(g * LANES, LANES), :] = jnp.broadcast_to(lrm[g:g + 1, :], (LANES, LANES)).T
    rf_cp.wait()
    eye = (lax.broadcasted_iota(jnp.int32, (rank, rank), 0)
           == lax.broadcasted_iota(jnp.int32, (rank, rank), 1)).astype(F32).astype(BF16)
    for i in range(chunks):
        rft[i] = lax.dot_general(eye, rf[pl.ds(i * rchunk, rchunk), :], NT,
                                 preferred_element_type=F32).astype(BF16)
    msum = rm_ref[...].astype(F32)
    for cp, k in zip(mar_cp, range(1, 2 * blks)):
        cp.wait_recv()
        msum = msum + mar[k].astype(F32)
    total = jnp.sum(jnp.sum(msum, axis=0, keepdims=True), axis=1, keepdims=True)
    log_total = jnp.log(jnp.broadcast_to(total, (1, LANES)))
    for s in range(slots):
        block = lax.rem(b + s - half + blks, blks)
        for t in range(tiles):
            at = (block * cols + c) * tiles + t
            ncl[s, pl.ds(t, 1), :] = jnp.log(cm_ref[pl.ds(at, 1), :].astype(F32)) - log_total

    cf_cp.wait()
    for cp in cnt_cp:
        cp.wait()

    def tile_work(i, s, first_rows):
        at = pl.ds(pl.multiple_of(i * rchunk, rchunk), rchunk)
        score = lax.dot_general(rf[at, :], cfb[s], NT, preferred_element_type=F32)
        lr = rb[at, :]
        halves = []
        for t in range(tiles):
            n = cnt[pl.ds(i * per_chunk + t * slots + s, rchunk, stride=tiles * slots), :].astype(F32)
            x = score[:, t * LANES:(t + 1) * LANES] + (lr + ncl[s, pl.ds(t, 1), :])
            conf = 0.1 * loss_scale + (0.25 * loss_scale) * (n * lax.rsqrt(n))
            seen = conf * (x - jnp.log(n))
            unseen = (0.5 * loss_scale) * jnp.tanh(0.5 * x) + 0.5 * loss_scale
            halves.append(jnp.where(n > 0.0, seen, unseen).astype(BF16))
        slope = jnp.concatenate(halves, axis=1)
        row_part = jnp.dot(slope, cfb[s], preferred_element_type=F32)
        col_part = jnp.dot(rft[i], slope, preferred_element_type=F32)
        return row_part, col_part

    def add_col(i, s, col_part):
        @pl.when(i == 0)
        def _():
            cacc[s] = col_part

        @pl.when(i > 0)
        def _():
            cacc[s] += col_part

    give = pl.ds(pl.multiple_of(other * hk, hk), hk)
    keep = pl.ds(pl.multiple_of(r * hk, hk), hk)
    rep_cp = {}

    def start_rep(s):
        cp = pltpu.make_async_remote_copy(
            src_ref=cacc.at[s, give], dst_ref=cin.at[s], send_sem=rep_s.at[s], recv_sem=rep_r.at[s],
            device_id={"rep": other}, device_id_type=MESH)
        cp.start()
        rep_cp[s] = cp
        sends.append(cp)

    z_cp = {}

    def start_z(s):
        rep_cp[s].wait_recv()
        if s == half:
            csum[...] = cacc[s, keep, :] + cin[s]
            return
        zout[s] = (cacc[s, keep, :] + cin[s]).astype(BF16)
        cp = pltpu.make_async_remote_copy(
            src_ref=zout.at[s], dst_ref=zin.at[s], send_sem=z_s.at[s], recv_sem=z_r.at[s],
            device_id={"blk": lax.rem(b + s - half + blks, blks)}, device_id_type=MESH)
        cp.start()
        z_cp[s] = cp
        sends.append(cp)

    fw_cp = {}

    def forward(s):
        cf_in[s].wait_recv()
        cp = pltpu.make_async_remote_copy(
            src_ref=cfb.at[s, my_half], dst_ref=cfb.at[s, my_half], send_sem=fw_s.at[s], recv_sem=fw_r.at[s],
            device_id={"rep": other}, device_id_type=MESH)
        cp.start()
        fw_cp[s] = cp
        sends.append(cp)

    @pl.loop(0, chunks)
    def _(i):
        row_part, col_part = tile_work(i, half, True)
        racc[pl.ds(pl.multiple_of(i * rchunk, rchunk), rchunk), :] = row_part
        add_col(i, half, col_part)

    start_rep(half)
    for s in others:
        forward(s)
    for s in others:
        fw_cp[s].wait_recv()
    start_z(half)

    def x_copy(i, k):
        at = pl.ds(pl.multiple_of(i * rchunk, rchunk), rchunk)
        return pltpu.make_async_remote_copy(
            src_ref=rbf.at[at], dst_ref=parts.at[c, at], send_sem=x_s.at[k - 1, i], recv_sem=x_r.at[k - 1, i],
            device_id={"col": lax.rem(c + k, cols)}, device_id_type=MESH)

    def own_copy(i):
        at = pl.ds(pl.multiple_of(i * rchunk, rchunk), rchunk)
        return pltpu.make_async_copy(rbf.at[at], parts.at[c, at], own_sem.at[i])

    @pl.loop(0, chunks)
    def _(i):
        at = pl.ds(pl.multiple_of(i * rchunk, rchunk), rchunk)
        acc = racc[at, :]
        for s in others:
            row_part, col_part = tile_work(i, s, False)
            acc = acc + row_part
            add_col(i, s, col_part)
        rbf[at, :] = acc.astype(BF16)
        for k in range(1, cols):
            x_copy(i, k).start()
        own_copy(i).start()

    for s in others:
        start_rep(s)
    for s in others:
        start_z(s)
    acc = csum[...]
    for s in others:
        z_cp[s].wait_recv()
        acc = acc + zin[s].astype(F32)
    lane_half = pl.ds(pl.multiple_of(r * hk, hk), hk)
    outv[:, lane_half] = acc.T
    fin = pltpu.make_async_remote_copy(
        src_ref=outv.at[:, lane_half], dst_ref=outv.at[:, lane_half], send_sem=fin_s, recv_sem=fin_r,
        device_id={"rep": other}, device_id_type=MESH)
    fin.start()
    fin.wait_recv()
    out_cp = pltpu.make_async_copy(outv, colout, loc_sem.at[0])
    out_cp.start()
    for i in range(chunks):
        own_copy(i).wait()
        for k in range(1, cols):
            x_copy(i, k).wait()
    for cp in sends:
        cp.wait_send()
    fin.wait_send()
    out_cp.wait()


def per_device(blks, cols, row_factors, col_factors, counts, row_margin, col_margin):
    rows, rank = row_factors.shape
    piece = col_factors.shape[0]
    slots = counts.shape[1]
    tiles = piece // LANES
    rchunk = 256
    chunks = rows // rchunk
    flat = counts.reshape(rows, slots, tiles, LANES).transpose(0, 2, 1, 3).reshape(rows * tiles * slots, LANES)
    rm = row_margin.reshape(rows // LANES, LANES)
    cm = col_margin.reshape(-1, LANES)
    dma = pltpu.SemaphoreType.DMA
    vmem = pltpu.VMEM
    anyspec = pl.BlockSpec(memory_space=pl.ANY)
    vspec = pl.BlockSpec(memory_space=pltpu.VMEM)
    cells = rows * piece * slots
    parts, col_grad = pl.pallas_call(
        functools.partial(kernel, (blks, cols, slots, rchunk)),
        out_shape=(jax.ShapeDtypeStruct((cols, rows, rank), BF16),
                   jax.ShapeDtypeStruct((piece, rank), F32)),
        in_specs=[anyspec, anyspec, anyspec, vspec, vspec],
        out_specs=(anyspec, anyspec),
        scratch_shapes=[
            vmem((rows, rank), BF16),
            vmem((slots, piece, rank), BF16),
            vmem((rows * tiles * slots, LANES), jnp.int32),
            vmem((2 * blks, rows // LANES, LANES), jnp.int32),
            vmem((chunks, rank, rchunk), BF16),
            vmem((rows, LANES), F32),
            vmem((slots, tiles, LANES), F32),
            vmem((rows, rank), F32),
            vmem((rows, rank), BF16),
            vmem((slots, rank, piece), F32),
            vmem((slots, rank // 2, piece), F32),
            vmem((rank // 2, piece), F32),
            vmem((slots, rank // 2, piece), BF16),
            vmem((slots, rank // 2, piece), BF16),
            vmem((piece, rank), F32),
            dma((chunks,)), dma((2,)),
            dma((2 * blks,)), dma((2 * blks,)),
            dma((slots,)), dma((slots,)), dma((slots,)), dma((slots,)),
            dma((slots,)), dma((slots,)), dma((slots,)), dma((slots,)),
            dma((max(cols - 1, 1), chunks)), dma((max(cols - 1, 1), chunks)),
            dma((chunks,)), dma, dma,
        ],
        compiler_params=pltpu.CompilerParams(
            collective_id=0, has_side_effects=True, vmem_limit_bytes=44 * 1024 * 1024),
        cost_estimate=pl.CostEstimate(
            flops=6 * cells * rank, bytes_accessed=4 * cells, transcendentals=3 * cells),
    )(row_factors, col_factors, flat, rm, cm)
    return jnp.sum(parts.astype(F32), axis=0), col_grad


def solution(mesh):
    in_specs = (
        P(("groups", "blk", "rep"), None),
        P(("groups", "blk", "col"), None),
        P(("groups", "blk", "rep"), None, "col"),
        P(("groups", "blk", "rep")),
        P("groups"),
    )
    out_specs = (P(("groups", "blk", "rep"), None), P(("groups", "blk", "col"), None))
    body = functools.partial(per_device, mesh.shape["blk"], mesh.shape["col"])
    return jax.shard_map(body, mesh=mesh, in_specs=in_specs, out_specs=out_specs, check_vma=False)
```

time: 177 us -> 38 us (0.21)
  waiting for transfers between devices: 115 us -> 0 us
  Pallas kernels: 0 us -> 29.7 us
  blocking collectives: 15 us -> 0 us
  between operations: 15 us -> 0.65 us
  local copies, waits for them, and re-layouts: 16.2 us -> 6.21 us
  matrix products: 8.77 us -> 0 us
  starting transfers between devices: 5.39 us -> 0 us
    psum x2 -> x0, waiting for transfers between devices: 59.5 us -> none  [the longest x1 44.2 us: per_device(): row_grad = lax.psum(row_total, 'col')]
    ppermute x8 -> x0, waiting for transfers between devices: 55.1 us -> none  [passed_along(): lax.ppermute(value, axis, [(i, (i + by) % devices) for i in range(devices)])]
    pallas_call x0 -> x1, Pallas kernels: none -> 29.7 us  [per_device(): pl.pallas_call(functools.partial(kernel, (blks, cols, slots, rchunk)), ou...]
    psum x1 -> x0, blocking collectives: 15 us -> none  [per_device(): lax.psum(jnp.sum(row_margin.astype(jnp.float32)), ('blk', 'rep'))]
    slice x1 -> x0, local copies, waits for them, and re-layouts: 11.5 us -> none  [per_device(): tile_counts = counts[:, offset + half_steps, :]]
    dot_general x12 -> x0, matrix products: 8.77 us -> none  [the longest x4 5.27 us: per_device(): lax.dot_general(row_factors, carried_factors, (((1,), (1,)), ((), ())), p...]
    ppermute x8 -> x0, starting transfers between devices: 5.31 us -> none  [passed_along(): lax.ppermute(value, axis, [(i, (i + by) % devices) for i in range(devices)])]
    unnamed x12 -> x11, local copies, waits for them, and re-layouts: 4.66 us -> 6.21 us
  transfers between devices with their start and end apart: 10 -> 0, of which waited for: 9 -> 0; matrix products, arithmetic and copies ran while one was open for 9% -> 0% of each run, Pallas kernels for 0% -> 0%
where the time goes in v1:
time: 38 us; the launch traced here: 37.7 us
  Pallas kernels  29.7 us (78%)
  local copies, waits for them, and re-layouts  6.21 us (16%)
  other arithmetic  1.14 us (3%)
  between operations  0.65 us (2%)
    pallas_call x1, Pallas kernels, per_device(): pl.pallas_call(functools.partial(kernel, (blks, cols, slots, rchunk)), ou...  29.7 us
    unnamed x11, local copies, waits for them, and re-layouts  6.21 us
    reduce_sum x1, other arithmetic, per_device(): return (jnp.sum(parts.astype(F32), axis=0), col_grad)  1.14 us

profile of v1, /device:TPU:0, one launch (start us, length us, event | category | flops | bytes accessed | tf_op | source)
XLA Modules:
  0.0 37.7 jit_solution(6566111686116300219)
XLA Ops:
  0.6 0.0 copy-start
  0.6 2.2 %copy-done = s32[1024,4,256]{2,1,0:T(4,128)S(1)} copy-done((s32[1024,4,256]{2,1,0:T(4,128)S(1)}, s32[1024,4,256]{2,1,0:T(4,128)}, u32[]{:S(2)}) %copy-start) | copy-done | bytes 4194328
  2.8 0.0 copy-start.1
  2.8 1.0 %copy-done.1 = bf16[1024,256]{1,0:T(8,128)(2,1)S(1)} copy-done((bf16[1024,256]{1,0:T(8,128)(2,1)S(1)}, bf16[1024,256]{1,0:T(8,128)(2,1)}, u32[]{:S(2)}) %copy-start.1) | copy-done | bytes 524312
  3.9 0.0 copy-start.2
  3.9 0.9 %copy-done.2 = bf16[256,256]{1,0:T(8,128)(2,1)S(1)} copy-done((bf16[256,256]{1,0:T(8,128)(2,1)S(1)}, bf16[256,256]{1,0:T(8,128)(2,1)}, u32[]{:S(2)}) %copy-start.2) | copy-done | bytes 131096
  4.8 0.0 copy-start.3
  4.8 0.7 %copy-done.3 = s32[2048]{0:T(1024)S(1)} copy-done((s32[2048]{0:T(1024)S(1)}, s32[2048]{0:T(1024)}, u32[]{:S(2)}) %copy-start.3) | copy-done | bytes 8216
  5.5 0.0 copy-start.4
  5.5 0.7 %copy-done.4 = s32[1024]{0:T(1024)S(1)} copy-done((s32[1024]{0:T(1024)S(1)}, s32[1024]{0:T(1024)}, u32[]{:S(2)}) %copy-start.4) | copy-done | bytes 4120
  6.2 29.7 %shard_map.68 = (bf16[2,1024,256]{2,1,0:T(8,128)(2,1)S(1)}, f32[256,256]{1,0:T(8,128)S(1)}) custom-call(bf16[1024,256]{1,0:T(8,128)(2,1)S(1)} %copy-done.1, bf16[256,256]{1,0:T(8,128)(2,1)S(1)} %copy-done.2, s32[8192,128]{1,0:T(8,128)S(1)} %bitcast.7, s32[8,128]{1,0:T(8,128)S(1)} %bitcast.9, s32[16,128]{1,0:T(8,128)S(1)} %bitcast.8), custom_call_target="tpu_custom_call" | custom-call | flops 1610612736 | bytes 4194304 | tf_op jit(solution)/shard_map/pallas_call | solution.py:248
  35.9 1.1 %convert_reduce_fusion = f32[1024,256]{1,0:T(8,128)} fusion(bf16[2,1024,256]{2,1,0:T(8,128)(2,1)S(1)} %get-tuple-element.4), kind=kLoop, calls=%fused_computation | loop fusion | flops 786432 | bytes 2097152 | tf_op jit(solution)/shard_map/reduce_sum | solution.py:282
  37.0 0.7 %copy.9 = f32[256,256]{1,0:T(8,128)} copy(f32[256,256]{1,0:T(8,128)S(1)} %get-tuple-element.9) | data formatting | bytes 524288
Async XLA Ops:
  0.6 2.2 %copy-start = (s32[1024,4,256]{2,1,0:T(4,128)S(1)}, s32[1024,4,256]{2,1,0:T(4,128)}, u32[]{:S(2)}) copy-start(s32[1024,4,256]{2,1,0:T(4,128)} %param.7) | copy-start | bytes 12582916
  2.8 1.0 %copy-start.1 = (bf16[1024,256]{1,0:T(8,128)(2,1)S(1)}, bf16[1024,256]{1,0:T(8,128)(2,1)}, u32[]{:S(2)}) copy-start(bf16[1024,256]{1,0:T(8,128)(2,1)} %rf_hbm.1) | copy-start | bytes 1572868
  3.9 0.9 %copy-start.2 = (bf16[256,256]{1,0:T(8,128)(2,1)S(1)}, bf16[256,256]{1,0:T(8,128)(2,1)}, u32[]{:S(2)}) copy-start(bf16[256,256]{1,0:T(8,128)(2,1)} %cf_hbm.1) | copy-start | bytes 393220
  4.8 0.7 %copy-start.3 = (s32[2048]{0:T(1024)S(1)}, s32[2048]{0:T(1024)}, u32[]{:S(2)}) copy-start(s32[2048]{0:T(1024)} %param.9) | copy-start | bytes 24580
  5.5 0.7 %copy-start.4 = (s32[1024]{0:T(1024)S(1)}, s32[1024]{0:T(1024)}, u32[]{:S(2)}) copy-start(s32[1024]{0:T(1024)} %param.8) | copy-start | bytes 12292

commit v2 on v1

--- a/solution.py
+++ b/solution.py
@@ -10,13 +10,14 @@
 MESH = pl.DeviceIdType.MESH
 F32 = jnp.float32
 BF16 = jnp.bfloat16
+FIN = 60
 NT = (((1,), (1,)), ((), ()))
 LANES = 128
 
 
-def kernel(dims, rf_hbm, cf_hbm, cnt_hbm, rm_ref, cm_ref,
+def kernel(dims, rf_hbm, cf_hbm, cnt_hbm, rm_hbm, cm_hbm,
            parts, colout,
-           rf, cfb, cnt, mar, rft, rb, ncl, racc, rbf, cacc, cin, csum, zout, zin, outv,
+           rf, cfb, cnt, rm_ref, cm_ref, mar, rft, rb, ncl, racc, rbf, cacc, cin, csum, zout, zin, outv,
            cnt_sem, loc_sem, mar_s, mar_r, cf_s, cf_r, fw_s, fw_r,
            rep_s, rep_r, z_s, z_r, x_s, x_r, own_sem, fin_s, fin_r):
     blks, cols, slots, rchunk = dims
@@ -32,7 +33,10 @@
     r = lax.axis_index("rep")
     other = 1 - r
     loss_scale = float(slots * piece * cols) ** (-0.5)
-    others = sorted([s for s in range(slots) if s != half], key=lambda s: abs(s - half))
+    near = jnp.where(b == 0, half + 1, half - 1)
+    others = [near, 2 * half - near] + sorted(
+        [s for s in range(slots) if abs(s - half) > 1], key=lambda s: abs(s - half))
+    last = range(len(others))
     per_chunk = rchunk * tiles * slots
 
     bar = pltpu.get_barrier_semaphore()
@@ -44,6 +48,10 @@
     for k in range(1, cols):
         pl.semaphore_signal(bar, inc=1, device_id={"col": lax.rem(c + k, cols)}, device_id_type=MESH)
 
+    rm_cp = pltpu.make_async_copy(rm_hbm, rm_ref, loc_sem.at[2])
+    rm_cp.start()
+    cm_cp = pltpu.make_async_copy(cm_hbm, cm_ref, loc_sem.at[3])
+    cm_cp.start()
     rf_cp = pltpu.make_async_copy(rf_hbm, rf, loc_sem.at[0])
     rf_cp.start()
     cf_cp = pltpu.make_async_copy(cf_hbm, cfb.at[half], loc_sem.at[1])
@@ -63,21 +71,23 @@
             if d or e:
                 k = d * 2 + e
                 cp = pltpu.make_async_remote_copy(
-                    src_ref=rm_ref, dst_ref=mar.at[k], send_sem=mar_s.at[k], recv_sem=mar_r.at[k],
+                    src_ref=rm_hbm, dst_ref=mar.at[k], send_sem=mar_s.at[k], recv_sem=mar_r.at[k],
                     device_id={"blk": lax.rem(b + d, blks), "rep": lax.rem(r + e, 2)}, device_id_type=MESH)
                 cp.start()
                 mar_cp.append(cp)
     sends += mar_cp
     my_half = pl.ds(pl.multiple_of(r * hp, hp), hp)
-    cf_in = {}
+    cf_in = []
     for s in others:
         cp = pltpu.make_async_remote_copy(
             src_ref=cf_hbm.at[my_half], dst_ref=cfb.at[s, my_half], send_sem=cf_s.at[s], recv_sem=cf_r.at[s],
             device_id={"blk": lax.rem(b - s + half + blks, blks)}, device_id_type=MESH)
         cp.start()
-        cf_in[s] = cp
-    sends += list(cf_in.values())
-
+        cf_in.append(cp)
+    sends += cf_in
+
+    rm_cp.wait()
+    cm_cp.wait()
     lrm = jnp.log(rm_ref[...].astype(F32))
     for g in range(rows // LANES):
         rb[pl.ds(g * LANES, LANES), :] = jnp.broadcast_to(lrm[g:g + 1, :], (LANES, LANES)).T
@@ -131,54 +141,63 @@
 
     give = pl.ds(pl.multiple_of(other * hk, hk), hk)
     keep = pl.ds(pl.multiple_of(r * hk, hk), hk)
-    rep_cp = {}
-
-    def start_rep(s):
-        cp = pltpu.make_async_remote_copy(
+
+    def rep_copy(s):
+        return pltpu.make_async_remote_copy(
             src_ref=cacc.at[s, give], dst_ref=cin.at[s], send_sem=rep_s.at[s], recv_sem=rep_r.at[s],
             device_id={"rep": other}, device_id_type=MESH)
-        cp.start()
-        rep_cp[s] = cp
+
+    def start_rep(s):
+        cp = rep_copy(s)
+        cp.start()
         sends.append(cp)
 
-    z_cp = {}
-
-    def start_z(s):
-        rep_cp[s].wait_recv()
-        if s == half:
-            csum[...] = cacc[s, keep, :] + cin[s]
-            return
-        zout[s] = (cacc[s, keep, :] + cin[s]).astype(BF16)
-        cp = pltpu.make_async_remote_copy(
+    def z_copy(s):
+        return pltpu.make_async_remote_copy(
             src_ref=zout.at[s], dst_ref=zin.at[s], send_sem=z_s.at[s], recv_sem=z_r.at[s],
             device_id={"blk": lax.rem(b + s - half + blks, blks)}, device_id_type=MESH)
-        cp.start()
-        z_cp[s] = cp
+
+    def start_z(s):
+        rep_copy(s).wait_recv()
+        zout[s] = (cacc[s, keep, :] + cin[s]).astype(BF16)
+        cp = z_copy(s)
+        cp.start()
         sends.append(cp)
 
-    fw_cp = {}
-
-    def forward(s):
-        cf_in[s].wait_recv()
-        cp = pltpu.make_async_remote_copy(
+    def fw_copy(s):
+        return pltpu.make_async_remote_copy(
             src_ref=cfb.at[s, my_half], dst_ref=cfb.at[s, my_half], send_sem=fw_s.at[s], recv_sem=fw_r.at[s],
             device_id={"rep": other}, device_id_type=MESH)
-        cp.start()
-        fw_cp[s] = cp
+
+    def forward(n):
+        cf_in[n].wait_recv()
+        cp = fw_copy(others[n])
+        cp.start()
         sends.append(cp)
 
-    @pl.loop(0, chunks)
-    def _(i):
+    def own_rows(i):
         row_part, col_part = tile_work(i, half, True)
         racc[pl.ds(pl.multiple_of(i * rchunk, rchunk), rchunk), :] = row_part
         add_col(i, half, col_part)
 
+    def near_rows(i):
+        row_part, col_part = tile_work(i, near, False)
+        racc[pl.ds(pl.multiple_of(i * rchunk, rchunk), rchunk), :] += row_part
+        add_col(i, near, col_part)
+
+    pl.loop(0, chunks // 2)(own_rows)
+    forward(0)
+    pl.loop(chunks // 2, chunks)(own_rows)
     start_rep(half)
-    for s in others:
-        forward(s)
-    for s in others:
-        fw_cp[s].wait_recv()
-    start_z(half)
+    forward(1)
+    fw_copy(others[0]).wait_recv()
+    pl.loop(0, chunks // 2)(near_rows)
+    for n in last[2:]:
+        forward(n)
+    pl.loop(chunks // 2, chunks)(near_rows)
+    start_rep(near)
+    for n in last[1:]:
+        fw_copy(others[n]).wait_recv()
 
     def x_copy(i, k):
         at = pl.ds(pl.multiple_of(i * rchunk, rchunk), rchunk)
@@ -190,11 +209,10 @@
         at = pl.ds(pl.multiple_of(i * rchunk, rchunk), rchunk)
         return pltpu.make_async_copy(rbf.at[at], parts.at[c, at], own_sem.at[i])
 
-    @pl.loop(0, chunks)
-    def _(i):
+    def rest_rows(i):
         at = pl.ds(pl.multiple_of(i * rchunk, rchunk), rchunk)
         acc = racc[at, :]
-        for s in others:
+        for s in others[1:]:
             row_part, col_part = tile_work(i, s, False)
             acc = acc + row_part
             add_col(i, s, col_part)
@@ -203,13 +221,19 @@
             x_copy(i, k).start()
         own_copy(i).start()
 
-    for s in others:
+    pl.loop(0, 1)(rest_rows)
+    start_z(near)
+    pl.loop(1, chunks)(rest_rows)
+
+    for s in others[1:]:
         start_rep(s)
-    for s in others:
+    rep_copy(half).wait_recv()
+    csum[...] = cacc[half, keep, :] + cin[half]
+    for s in others[1:]:
         start_z(s)
     acc = csum[...]
     for s in others:
-        z_cp[s].wait_recv()
+        z_copy(s).wait_recv()
         acc = acc + zin[s].astype(F32)
     lane_half = pl.ds(pl.multiple_of(r * hk, hk), hk)
     outv[:, lane_half] = acc.T
@@ -230,6 +254,46 @@
     out_cp.wait()
 
 
+def finish_kernel(parts, col, row_out, col_out, pin, vout, cv, in_sem, out_sem, col_sem):
+    cols, rows = parts.shape[0], parts.shape[1]
+    step = rows // 4
+    col_in = pltpu.make_async_copy(col, cv, col_sem.at[0])
+    col_cp = pltpu.make_async_copy(cv, col_out, col_sem.at[1])
+    at = [pl.ds(i * step, step) for i in range(4)]
+    ins = [pltpu.make_async_copy(parts.at[:, a], pin.at[:, a], in_sem.at[i]) for i, a in enumerate(at)]
+    outs = [pltpu.make_async_copy(vout.at[a], row_out.at[a], out_sem.at[i]) for i, a in enumerate(at)]
+    for cp in ins:
+        cp.start()
+    col_in.start()
+    for i, a in enumerate(at):
+        ins[i].wait()
+        acc = pin[0, a].astype(F32)
+        for k in range(1, cols):
+            acc = acc + pin[k, a].astype(F32)
+        vout[a] = acc
+        outs[i].start()
+    col_in.wait()
+    col_cp.start()
+    for cp in outs:
+        cp.wait()
+    col_cp.wait()
+
+
+def finish(parts, col):
+    dma = pltpu.SemaphoreType.DMA
+    anyspec = pl.BlockSpec(memory_space=pl.ANY)
+    hspec = pl.BlockSpec(memory_space=pltpu.HBM)
+    return pl.pallas_call(
+        finish_kernel,
+        out_shape=(jax.ShapeDtypeStruct(parts.shape[1:], F32), jax.ShapeDtypeStruct(col.shape, F32)),
+        in_specs=[anyspec, anyspec],
+        out_specs=(hspec, hspec),
+        scratch_shapes=[pltpu.VMEM(parts.shape, BF16), pltpu.VMEM(parts.shape[1:], F32),
+                        pltpu.VMEM(col.shape, F32), dma((4,)), dma((4,)), dma((2,))],
+        compiler_params=pltpu.CompilerParams(vmem_limit_bytes=FIN * 1024 * 1024),
+    )(parts, col)
+
+
 def per_device(blks, cols, row_factors, col_factors, counts, row_margin, col_margin):
     rows, rank = row_factors.shape
     piece = col_factors.shape[0]
@@ -243,18 +307,20 @@
     dma = pltpu.SemaphoreType.DMA
     vmem = pltpu.VMEM
     anyspec = pl.BlockSpec(memory_space=pl.ANY)
-    vspec = pl.BlockSpec(memory_space=pltpu.VMEM)
+    hspec = pl.BlockSpec(memory_space=pltpu.HBM)
     cells = rows * piece * slots
     parts, col_grad = pl.pallas_call(
         functools.partial(kernel, (blks, cols, slots, rchunk)),
         out_shape=(jax.ShapeDtypeStruct((cols, rows, rank), BF16),
                    jax.ShapeDtypeStruct((piece, rank), F32)),
-        in_specs=[anyspec, anyspec, anyspec, vspec, vspec],
+        in_specs=[hspec] * 5,
         out_specs=(anyspec, anyspec),
         scratch_shapes=[
             vmem((rows, rank), BF16),
             vmem((slots, piece, rank), BF16),
             vmem((rows * tiles * slots, LANES), jnp.int32),
+            vmem(rm.shape, jnp.int32),
+            vmem(cm.shape, jnp.int32),
             vmem((2 * blks, rows // LANES, LANES), jnp.int32),
             vmem((chunks, rank, rchunk), BF16),
             vmem((rows, LANES), F32),
@@ -267,7 +333,7 @@
             vmem((slots, rank // 2, piece), BF16),
             vmem((slots, rank // 2, piece), BF16),
             vmem((piece, rank), F32),
-            dma((chunks,)), dma((2,)),
+            dma((chunks,)), dma((4,)),
             dma((2 * blks,)), dma((2 * blks,)),
             dma((slots,)), dma((slots,)), dma((slots,)), dma((slots,)),
             dma((slots,)), dma((slots,)), dma((slots,)), dma((slots,)),
@@ -275,11 +341,11 @@
             dma((chunks,)), dma, dma,
         ],
         compiler_params=pltpu.CompilerParams(
-            collective_id=0, has_side_effects=True, vmem_limit_bytes=44 * 1024 * 1024),
+            collective_id=0, has_side_effects=True, vmem_limit_bytes=62 * 1024 * 1024),
         cost_estimate=pl.CostEstimate(
             flops=6 * cells * rank, bytes_accessed=4 * cells, transcendentals=3 * cells),
     )(row_factors, col_factors, flat, rm, cm)
-    return jnp.sum(parts.astype(F32), axis=0), col_grad
+    return finish(parts, col_grad)
 
 
 def solution(mesh):

time: 38 us -> 32.3 us (0.85)
  local copies, waits for them, and re-layouts: 6.21 us -> 0 us
  Pallas kernels: 29.7 us -> 31.5 us
  other arithmetic: 1.14 us -> 0 us
    unnamed x11 -> x0, local copies, waits for them, and re-layouts: 6.21 us -> none
    pallas_call x0 -> x1, Pallas kernels: none -> 2.11 us  [finish(): pl.pallas_call(finish_kernel, out_shape=(jax.ShapeDtypeStruct(parts.shape...]
    reduce_sum x1 -> x0, other arithmetic: 1.14 us -> none  [per_device(): return (jnp.sum(parts.astype(F32), axis=0), col_grad)]
    pallas_call x1, Pallas kernels: 29.7 us -> 29.4 us  [per_device(): pl.pallas_call(functools.partial(kernel, (blks, cols, slots, rchunk)), ou...]
where the time goes in v2:
time: 32.3 us; the launch traced here: 32.1 us
  Pallas kernels  31.5 us (98%)
  between operations  0.64 us (2%)
    pallas_call x1, Pallas kernels, per_device(): pl.pallas_call(functools.partial(kernel, (blks, cols, slots, rchunk)), ou...  29.4 us
    pallas_call x1, Pallas kernels, finish(): pl.pallas_call(finish_kernel, out_shape=(jax.ShapeDtypeStruct(parts.shape...  2.11 us

profile of v2, /device:TPU:0, one launch (start us, length us, event | category | flops | bytes accessed | tf_op | source)
XLA Modules:
  0.0 32.1 jit_solution(699992425633006298)
XLA Ops:
  0.6 29.4 %shard_map.68 = (bf16[2,1024,256]{2,1,0:T(8,128)(2,1)}, f32[256,256]{1,0:T(8,128)}) custom-call(bf16[1024,256]{1,0:T(8,128)(2,1)} %rf_hbm.1, bf16[256,256]{1,0:T(8,128)(2,1)} %cf_hbm.1, s32[8192,128]{1,0:T(8,128)} %bitcast.7, s32[8,128]{1,0:T(8,128)} %bitcast.9, s32[16,128]{1,0:T(8,128)} %bitcast.8), custom_call_target="tpu_custom_call" | custom-call | flops 1610612736 | bytes 4194304 | tf_op jit(solution)/shard_map/pallas_call | solution.py:312
  30.0 2.1 %shard_map.69 = (f32[1024,256]{1,0:T(8,128)}, f32[256,256]{1,0:T(8,128)}) custom-call(bf16[2,1024,256]{2,1,0:T(8,128)(2,1)} %get-tuple-element.4.parts, f32[256,256]{1,0:T(8,128)} %get-tuple-element.5.col), custom_call_target="tpu_custom_call" | custom-call | tf_op jit(solution)/shard_map/pallas_call | solution.py:286

commit v3 on v2

--- a/solution.py
+++ b/solution.py
@@ -17,7 +17,7 @@
 
 def kernel(dims, rf_hbm, cf_hbm, cnt_hbm, rm_hbm, cm_hbm,
            parts, colout,
-           rf, cfb, cnt, rm_ref, cm_ref, mar, rft, rb, ncl, racc, rbf, cacc, cin, csum, zout, zin, outv,
+           rf, cfb, cnt, rm_ref, cm_ref, msrc, mar, rft, rb, ncl, racc, rbf, cacc, cin, csum, zout, zin, outv,
            cnt_sem, loc_sem, mar_s, mar_r, cf_s, cf_r, fw_s, fw_r,
            rep_s, rep_r, z_s, z_r, x_s, x_r, own_sem, fin_s, fin_r):
     blks, cols, slots, rchunk = dims
@@ -33,7 +33,7 @@
     r = lax.axis_index("rep")
     other = 1 - r
     loss_scale = float(slots * piece * cols) ** (-0.5)
-    near = jnp.where(b == 0, half + 1, half - 1)
+    near = jnp.where(b < blks // 2, half + 1, half - 1)
     others = [near, 2 * half - near] + sorted(
         [s for s in range(slots) if abs(s - half) > 1], key=lambda s: abs(s - half))
     last = range(len(others))
@@ -62,6 +62,9 @@
         cp = pltpu.make_async_copy(cnt_hbm.at[at], cnt.at[at], cnt_sem.at[i])
         cp.start()
         cnt_cp.append(cp)
+    rm_cp.wait()
+    own_sum = jnp.sum(rm_ref[...].astype(F32), axis=0, keepdims=True)
+    msrc[...] = own_sum
     pl.semaphore_wait(bar, 2 * blks - 1 + cols - 1)
 
     sends = []
@@ -71,22 +74,22 @@
             if d or e:
                 k = d * 2 + e
                 cp = pltpu.make_async_remote_copy(
-                    src_ref=rm_hbm, dst_ref=mar.at[k], send_sem=mar_s.at[k], recv_sem=mar_r.at[k],
+                    src_ref=msrc, dst_ref=mar.at[k], send_sem=mar_s.at[k], recv_sem=mar_r.at[k],
                     device_id={"blk": lax.rem(b + d, blks), "rep": lax.rem(r + e, 2)}, device_id_type=MESH)
                 cp.start()
                 mar_cp.append(cp)
     sends += mar_cp
     my_half = pl.ds(pl.multiple_of(r * hp, hp), hp)
     cf_in = []
-    for s in others:
+    for s in others[:1] + others[2:] + others[1:2]:
         cp = pltpu.make_async_remote_copy(
             src_ref=cf_hbm.at[my_half], dst_ref=cfb.at[s, my_half], send_sem=cf_s.at[s], recv_sem=cf_r.at[s],
             device_id={"blk": lax.rem(b - s + half + blks, blks)}, device_id_type=MESH)
         cp.start()
         cf_in.append(cp)
+    cf_in = cf_in[:1] + cf_in[-1:] + cf_in[1:-1]
     sends += cf_in
 
-    rm_cp.wait()
     cm_cp.wait()
     lrm = jnp.log(rm_ref[...].astype(F32))
     for g in range(rows // LANES):
@@ -97,11 +100,11 @@
     for i in range(chunks):
         rft[i] = lax.dot_general(eye, rf[pl.ds(i * rchunk, rchunk), :], NT,
                                  preferred_element_type=F32).astype(BF16)
-    msum = rm_ref[...].astype(F32)
+    msum = own_sum
     for cp, k in zip(mar_cp, range(1, 2 * blks)):
         cp.wait_recv()
-        msum = msum + mar[k].astype(F32)
-    total = jnp.sum(jnp.sum(msum, axis=0, keepdims=True), axis=1, keepdims=True)
+        msum = msum + mar[k]
+    total = jnp.sum(msum, axis=1, keepdims=True)
     log_total = jnp.log(jnp.broadcast_to(total, (1, LANES)))
     for s in range(slots):
         block = lax.rem(b + s - half + blks, blks)
@@ -185,16 +188,16 @@
         racc[pl.ds(pl.multiple_of(i * rchunk, rchunk), rchunk), :] += row_part
         add_col(i, near, col_part)
 
-    pl.loop(0, chunks // 2)(own_rows)
+    pl.loop(0, chunks // 2, unroll=True)(own_rows)
     forward(0)
-    pl.loop(chunks // 2, chunks)(own_rows)
+    pl.loop(chunks // 2, chunks, unroll=True)(own_rows)
     start_rep(half)
     forward(1)
     fw_copy(others[0]).wait_recv()
-    pl.loop(0, chunks // 2)(near_rows)
+    pl.loop(0, chunks // 2, unroll=True)(near_rows)
     for n in last[2:]:
         forward(n)
-    pl.loop(chunks // 2, chunks)(near_rows)
+    pl.loop(chunks // 2, chunks, unroll=True)(near_rows)
     start_rep(near)
     for n in last[1:]:
         fw_copy(others[n]).wait_recv()
@@ -321,7 +324,8 @@
             vmem((rows * tiles * slots, LANES), jnp.int32),
             vmem(rm.shape, jnp.int32),
             vmem(cm.shape, jnp.int32),
-            vmem((2 * blks, rows // LANES, LANES), jnp.int32),
+            vmem((1, LANES), F32),
+            vmem((2 * blks, 1, LANES), F32),
             vmem((chunks, rank, rchunk), BF16),
             vmem((rows, LANES), F32),
             vmem((slots, tiles, LANES), F32),

time: 32.3 us -> 31.1 us (0.963)
  Pallas kernels: 31.5 us -> 30.2 us
    pallas_call x1, Pallas kernels: 29.4 us -> 28.1 us  [per_device(): pl.pallas_call(functools.partial(kernel, (blks, cols, slots, rchunk)), ou...]
where the time goes in v3:
time: 31.1 us; the launch traced here: 30.9 us
  Pallas kernels  30.2 us (97%)
  between operations  0.64 us (2%)
    pallas_call x1, Pallas kernels, per_device(): pl.pallas_call(functools.partial(kernel, (blks, cols, slots, rchunk)), ou...  28.1 us
    pallas_call x1, Pallas kernels, finish(): pl.pallas_call(finish_kernel, out_shape=(jax.ShapeDtypeStruct(parts.shape...  2.11 us

profile of v3, /device:TPU:0, one launch (start us, length us, event | category | flops | bytes accessed | tf_op | source)
XLA Modules:
  0.0 30.9 jit_solution(10889937034451183107)
XLA Ops:
  0.6 28.1 %shard_map.68 = (bf16[2,1024,256]{2,1,0:T(8,128)(2,1)}, f32[256,256]{1,0:T(8,128)}) custom-call(bf16[1024,256]{1,0:T(8,128)(2,1)} %rf_hbm.1, bf16[256,256]{1,0:T(8,128)(2,1)} %cf_hbm.1, s32[8192,128]{1,0:T(8,128)} %bitcast.7, s32[8,128]{1,0:T(8,128)} %bitcast.9, s32[16,128]{1,0:T(8,128)} %bitcast.8), custom_call_target="tpu_custom_call" | custom-call | flops 1610612736 | bytes 4194304 | tf_op jit(solution)/shard_map/pallas_call | solution.py:315
  28.8 2.1 %shard_map.69 = (f32[1024,256]{1,0:T(8,128)}, f32[256,256]{1,0:T(8,128)}) custom-call(bf16[2,1024,256]{2,1,0:T(8,128)(2,1)} %get-tuple-element.4.parts, f32[256,256]{1,0:T(8,128)} %get-tuple-element.5.col), custom_call_target="tpu_custom_call" | custom-call | tf_op jit(solution)/shard_map/pallas_call | solution.py:289
